TPU v7x, 32 devices: a whole 2x2x4 slice. The times are simulated.
32 devices in a mesh: seq: 8 (over z, y), tp: 4 (over x, core).
Axes of the slice: x: 2, y: 2, z: 4, core: 2. Of those that a mesh axis runs over, the one named last changes fastest.
Arguments:
- probe_vectors: bfloat16 [4096, 8192], P('seq', 'tp'), may hold values from -6 to 6
- lookup_vectors: bfloat16 [4096, 8192], P('seq', 'tp'), may hold values from -0.5 to 0.5
- payload_vectors: bfloat16 [4096, 8192], P('seq', 'tp'), may hold values from -400 to 400
- attender_fading_pace: float32 [64], P('tp'), may hold values from 0 to 0.034, as said below
- surplus_fading: float32 [4096, 64], P('seq', 'tp'), may hold values from -0.7 to 0, as said below
- normalizer_scaling: float32 [8192], P('tp'), may hold values from 0.25 to 1.75
Outputs:
- attended: bfloat16 [4096, 8192], P('seq', 'tp')
- final_state: float32 [64, 16384], P('tp', 'seq')
Inputs may be any that keep to these rules, and one draw needn't show every extreme that they name: `attender_fading_pace`: positive per-token decay rates; some heads forget within some tens of tokens. `surplus_fading`: zero at most tokens.
All inputs are finite; a program needn't handle non-finite values.
Results may differ from a plain program's by a relative error of at most 0.0031.
Values sent between devices are 32-bit elements; how exact they have to be, the bound alone decides.
A program may use at most 192 MiB of HBM per device.

v0:
```python
import functools

import jax
import jax.numpy as jnp
from jax import lax
from jax.experimental import pallas as pl
from jax.experimental.pallas import tpu as pltpu
from jax.sharding import PartitionSpec as P

HEAD_DIM = 128
HALF = HEAD_DIM // 2
BLOCK = 256
D = 8192
EPS = 1e-06
LOG2E = 1.4426950408889634
F32 = jnp.float32
BF16 = jnp.bfloat16
MESH = pl.DeviceIdType.MESH


def split(x, axis):
    high = x.astype(BF16)
    low = (x - high.astype(F32)).astype(BF16)
    return jnp.concatenate([high, low], axis=axis)


def kernel(
    n, peers, heads, group,
    q_hbm, k_hbm, v_hbm, pace_ref, surplus_ref, gain_ref,
    out_hbm, final_ref,
    qs, ks, vs, outs, acc, crow, erow, krow, dblock, first, local, theirs, prior, before, after, give,
    dec, dec_theirs, fsend, frecv, squares,
    load_sem, store_sem, dec_sem, l_send, l_recv, p_send, p_recv, x_send, x_recv,
    f_send, f_recv, s_send, s_recv,
):
    tokens = q_hbm.shape[0]
    blocks = tokens // BLOCK
    chunks = heads // group
    wide = group * HEAD_DIM
    groups = n // 2
    rows = HEAD_DIM // n
    piece = max(rows, 8)
    me = lax.axis_index("seq")
    place = lax.axis_index("tp")
    g, r = me // 2, me % 2
    other = 1 - r
    partner = 2 * g + other

    def owner(s):
        top = s * rows
        return ((top // piece) * 2 * piece + r * piece + top % piece) // rows

    def halves(x):
        return [
            jnp.concatenate(
                [x[at : at + piece] for at in range(p * piece, HEAD_DIM, 2 * piece)], axis=0
            )
            for p in range(2)
        ]

    def joined(a, b):
        return jnp.concatenate(
            [x[at : at + piece] for at in range(0, HALF, piece) for x in (a, b)], axis=0
        )

    is_first, is_last = g == 0, g == groups - 1

    barrier = pltpu.get_barrier_semaphore()
    for step in range(1, n):
        pl.semaphore_signal(
            barrier, inc=1, device_id={"seq": lax.rem(me + step, n)}, device_id_type=MESH
        )
    for step in range(1, peers):
        pl.semaphore_signal(
            barrier, inc=1, device_id={"tp": lax.rem(place + step, peers)}, device_id_type=MESH
        )

    def lanes(i):
        return pl.ds(pl.multiple_of(i * wide, wide), wide)

    def load(which, i):
        source = (k_hbm, v_hbm, q_hbm)[which]
        target = (ks, vs, qs)[which]
        return pltpu.make_async_copy(
            source.at[:, lanes(i)], target.at[i], load_sem.at[which, i]
        )

    def store(i):
        return pltpu.make_async_copy(outs.at[i], out_hbm.at[:, lanes(i)], store_sem.at[i])

    def span(i):
        return pl.ds(i * group, group)

    def send_dec():
        return pltpu.make_async_remote_copy(
            src_ref=dec, dst_ref=dec_theirs, send_sem=dec_sem.at[0], recv_sem=dec_sem.at[1],
            device_id={"seq": partner}, device_id_type=MESH,
        )

    def send_local(i):
        return pltpu.make_async_remote_copy(
            src_ref=local.at[other, span(i)], dst_ref=theirs.at[span(i)],
            send_sem=l_send.at[i], recv_sem=l_recv.at[i],
            device_id={"seq": partner}, device_id_type=MESH,
        )

    def send_after(i):
        return pltpu.make_async_remote_copy(
            src_ref=after.at[span(i)], dst_ref=before.at[span(i)],
            send_sem=p_send.at[i], recv_sem=p_recv.at[i],
            device_id={"seq": lax.rem(me + 2, n)}, device_id_type=MESH,
        )

    def send_prior(i):
        return pltpu.make_async_remote_copy(
            src_ref=give.at[span(i)], dst_ref=prior.at[r, span(i)],
            send_sem=x_send.at[i], recv_sem=x_recv.at[i],
            device_id={"seq": partner}, device_id_type=MESH,
        )

    def send_final(i, s):
        return pltpu.make_async_remote_copy(
            src_ref=fsend.at[s, span(i)], dst_ref=frecv.at[span(i)],
            send_sem=f_send.at[i, s], recv_sem=f_recv.at[i],
            device_id={"seq": owner(s)}, device_id_type=MESH,
        )

    def send_squares(step):
        return pltpu.make_async_remote_copy(
            src_ref=squares.at[0], dst_ref=squares.at[step],
            send_sem=s_send.at[step], recv_sem=s_recv.at[step],
            device_id={"tp": lax.rem(place + step, peers)}, device_id_type=MESH,
        )

    for i in range(chunks):
        load(0, i).start()
        load(1, i).start()
    for i in range(chunks):
        load(2, i).start()

    square = (heads, heads)
    diagonal = lax.broadcasted_iota(jnp.int32, square, 0) == lax.broadcasted_iota(
        jnp.int32, square, 1
    )
    pace = jnp.sum(
        jnp.where(diagonal, jnp.broadcast_to(pace_ref[...], square), 0.0), axis=1, keepdims=True
    )
    logrows = surplus_ref[...] - pace
    upper = (
        lax.broadcasted_iota(jnp.int32, (BLOCK, BLOCK), 0)
        <= lax.broadcasted_iota(jnp.int32, (BLOCK, BLOCK), 1)
    ).astype(F32)
    total = jnp.zeros((heads, 1), F32)
    for b in range(blocks):
        at = slice(b * BLOCK, (b + 1) * BLOCK)
        c = lax.dot_general(
            logrows[:, at], upper, (((1,), (0,)), ((), ())),
            precision=lax.Precision.HIGHEST, preferred_element_type=F32,
        )
        last = c[:, BLOCK - 1 :]
        crow[:, at] = c * LOG2E
        erow[:, at] = jnp.exp(c)
        krow[:, at] = jnp.exp(last - c)
        total = total + last
        dblock[b] = jnp.exp(jnp.broadcast_to(last, (heads, HEAD_DIM)))
    decay = jnp.exp(jnp.broadcast_to(total, (heads, HEAD_DIM)))
    for h in range(heads):
        dec[h] = decay[h : h + 1, :]

    @pl.when(is_first)
    def _():
        before[...] = jnp.zeros_like(before)

        @pl.when(r == 0)
        def _():
            prior[1] = jnp.zeros(prior.shape[1:], F32)

    pl.semaphore_wait(barrier, n + peers - 2)
    send_dec().start()

    def make_local(i, carry):
        load(0, i).wait()
        load(1, i).wait()
        for e in range(group):
            h = i * group + e
            row = krow[pl.ds(h, 1), :]
            state = None
            for b in range(blocks):
                at = slice(b * BLOCK, (b + 1) * BLOCK)
                kt = ks[i, at, e * HEAD_DIM : (e + 1) * HEAD_DIM].astype(F32).T
                pair = jnp.dot(
                    split(kt * row[:, at], 0), vs[i, at, e * HEAD_DIM : (e + 1) * HEAD_DIM],
                    preferred_element_type=F32,
                )
                fresh = pair[:HEAD_DIM] + pair[HEAD_DIM:]
                state = fresh if b == 0 else dblock[b, pl.ds(h, 1), :] * state + fresh
                if b < blocks - 1:
                    first[b, h] = state
            local[0, h], local[1, h] = halves(state)
        send_local(i).start()
        return carry

    lax.fori_loop(0, chunks, make_local, 0)
    send_dec().wait_recv()

    def chain(i):
        send_local(i).wait_recv()

        @pl.when(jnp.logical_not(is_first))
        def _():
            send_after(i).wait_recv()

        at = span(i)
        mine, their = local[r, at], theirs[at]
        d_mine, d_their = dec[at], dec_theirs[at]
        came = before[at]
        even = r == 0
        grown = d_mine * d_their * came + jnp.where(
            even, d_their * mine + their, d_mine * their + mine
        )
        after[at] = grown

        @pl.when(jnp.logical_not(is_last))
        def _():
            send_after(i).start()

        prior[r, at] = jnp.where(even, came, d_their * came + their)

        give[at] = jnp.where(even, d_mine * came + mine, came)

        @pl.when(jnp.logical_not(is_first & (r == 1)))
        def _():
            send_prior(i).start()

        @pl.when(is_last)
        def _():
            for s in range(groups):
                fsend[s, at] = grown[:, s * rows : (s + 1) * rows, :]

            def give_final(s, carry):
                @pl.when(owner(s) != me)
                def _():
                    send_final(i, s).start()

                @pl.when(owner(s) == me)
                def _():
                    frecv[at] = fsend[s, at]

                return carry

            lax.fori_loop(0, groups, give_final, 0)

    side = BLOCK // 2
    lower = lax.broadcasted_iota(jnp.int32, (side, side), 0) >= lax.broadcasted_iota(
        jnp.int32, (side, side), 1
    )

    def intra(i):
        load(2, i).wait()
        for e in range(group):
            h = i * group + e
            cut = slice(e * HEAD_DIM, (e + 1) * HEAD_DIM)
            row = crow[pl.ds(h, 1), :]
            column = jnp.broadcast_to(row, (side, tokens)).T
            for b in range(blocks):
                at = slice(b * BLOCK, (b + 1) * BLOCK)
                scores = lax.dot_general(
                    qs[i, at, cut], ks[i, at, cut], (((1,), (1,)), ((), ())),
                    preferred_element_type=F32,
                )

                def weights(t, s):
                    rise = column[b * BLOCK + t : b * BLOCK + t + side, :] - (
                        row[:, b * BLOCK + s : b * BLOCK + s + side]
                    )
                    factor = jnp.exp2(rise)
                    if t == s:
                        factor = jnp.where(lower, factor, 0.0)
                    return (scores[t : t + side, s : s + side] * factor).astype(BF16)

                acc[h, b * BLOCK : b * BLOCK + side, :] = jnp.dot(
                    weights(0, 0), vs[i, b * BLOCK : b * BLOCK + side, cut],
                    preferred_element_type=F32,
                )
                acc[h, b * BLOCK + side : (b + 1) * BLOCK, :] = jnp.dot(
                    jnp.concatenate([weights(side, 0), weights(side, side)], axis=1),
                    vs[i, at, cut], preferred_element_type=F32,
                )

    lag = jnp.minimum(g, chunks)

    def middle(j, carry):
        @pl.when((j >= lag) & (j - lag < chunks))
        def _():
            chain(j - lag)

        @pl.when(j < chunks)
        def _():
            intra(j)

        return carry

    lax.fori_loop(0, chunks + min(groups - 1, chunks), middle, 0)

    def carried(i, sums):
        @pl.when(jnp.logical_not(is_first & (r == 0)))
        def _():
            send_prior(i).wait_recv()

        for e in range(group):
            h = i * group + e
            cut = slice(e * HEAD_DIM, (e + 1) * HEAD_DIM)
            start = joined(prior[0, h], prior[1, h])
            grows = jnp.broadcast_to(erow[pl.ds(h, 1), :], (HEAD_DIM, tokens)).T
            decayed = None
            parts = []
            for b in range(blocks):
                at = slice(b * BLOCK, (b + 1) * BLOCK)
                if b == 0:
                    state = start
                else:
                    state = decayed * start + first[b - 1, h]
                grow = grows[at]
                last = dblock[b, pl.ds(h, 1), :]
                decayed = last if b == 0 else decayed * last
                qb = qs[i, at, cut]
                inter = jnp.dot(
                    jnp.concatenate([qb, qb], axis=1), split(state, 0),
                    preferred_element_type=F32,
                )
                out = acc[h, at, :] + grow * inter
                acc[h, at, :] = out
                parts.append(out * out)
            sums = sums + jnp.concatenate(parts, axis=0)
        return sums

    sums = lax.fori_loop(0, chunks, carried, jnp.zeros((tokens, HEAD_DIM), F32))
    squares[0] = jnp.sum(sums.T, axis=0, keepdims=True)
    for step in range(1, peers):
        send_squares(step).start()
    for step in range(1, peers):
        send_squares(step).wait_recv()
    whole = squares[0]
    for step in range(1, peers):
        whole = whole + squares[step]
    scale = lax.rsqrt(whole / D + EPS)
    scale = jnp.broadcast_to(scale, (HEAD_DIM, tokens)).T

    def finish(i, carry):
        for e in range(group):
            h = i * group + e
            gain = gain_ref[:, pl.ds(pl.multiple_of(h * HEAD_DIM, HEAD_DIM), HEAD_DIM)]
            outs[i, :, e * HEAD_DIM : (e + 1) * HEAD_DIM] = (acc[h] * scale * gain).astype(BF16)
        store(i).start()
        return carry

    lax.fori_loop(0, chunks, finish, 0)

    def drain(i, carry):
        send_local(i).wait_send()

        @pl.when(jnp.logical_not(is_last))
        def _():
            send_after(i).wait_send()

        @pl.when(jnp.logical_not(is_first & (r == 1)))
        def _():
            send_prior(i).wait_send()

        @pl.when(is_last)
        def _():
            def sent(s, carry):
                @pl.when(owner(s) != me)
                def _():
                    send_final(i, s).wait_send()

                return carry

            lax.fori_loop(0, groups, sent, 0)

        @pl.when(jnp.logical_not(is_last & ((me * rows // piece) % 2 == r)))
        def _():
            send_final(i, 0).wait_recv()

        store(i).wait()
        return carry

    lax.fori_loop(0, chunks, drain, 0)
    send_dec().wait_send()
    for step in range(1, peers):
        send_squares(step).wait_send()
    for at in range(rows):
        final_ref[:, at * HEAD_DIM : (at + 1) * HEAD_DIM] = frecv[:, at, :]


def on_device(n, peers, q, k, v, pace, surplus, gain):
    tokens, width = q.shape
    heads = pace.shape[0]
    group = 2
    chunks = heads // group
    blocks = tokens // BLOCK
    groups = n // 2
    rows = HEAD_DIM // n
    vmem = pltpu.VMEM
    dma = pltpu.SemaphoreType.DMA
    half = (heads, HALF, HEAD_DIM)
    flops = 2 * heads * tokens * HEAD_DIM * (2 * BLOCK + 4 * HEAD_DIM)
    return pl.pallas_call(
        functools.partial(kernel, n, peers, heads, group),
        out_shape=(
            jax.ShapeDtypeStruct((tokens, width), BF16),
            jax.ShapeDtypeStruct((heads, rows * HEAD_DIM), F32),
        ),
        in_specs=[pl.BlockSpec(memory_space=pl.ANY)] * 3
        + [pl.BlockSpec(memory_space=pltpu.VMEM)] * 3,
        out_specs=(
            pl.BlockSpec(memory_space=pl.ANY),
            pl.BlockSpec(memory_space=pltpu.VMEM),
        ),
        scratch_shapes=[
            vmem((chunks, tokens, group * HEAD_DIM), BF16),
            vmem((chunks, tokens, group * HEAD_DIM), BF16),
            vmem((chunks, tokens, group * HEAD_DIM), BF16),
            vmem((chunks, tokens, group * HEAD_DIM), BF16),
            vmem((heads, tokens, HEAD_DIM), F32),
            vmem((heads, tokens), F32),
            vmem((heads, tokens), F32),
            vmem((heads, tokens), F32),
            vmem((blocks, heads, HEAD_DIM), F32),
            vmem((max(blocks - 1, 1), heads, HEAD_DIM, HEAD_DIM), F32),
            vmem((2,) + half, F32),
            vmem(half, F32),
            vmem((2,) + half, F32),
            vmem(half, F32),
            vmem(half, F32),
            vmem(half, F32),
            vmem((heads, 1, HEAD_DIM), F32),
            vmem((heads, 1, HEAD_DIM), F32),
            vmem((groups, heads, rows, HEAD_DIM), F32),
            vmem((heads, rows, HEAD_DIM), F32),
            vmem((peers, 1, tokens), F32),
            dma((3, chunks)),
            dma((chunks,)),
            dma((2,)),
            dma((chunks,)),
            dma((chunks,)),
            dma((chunks,)),
            dma((chunks,)),
            dma((chunks,)),
            dma((chunks,)),
            dma((chunks, groups)),
            dma((chunks,)),
            dma((peers,)),
            dma((peers,)),
        ],
        compiler_params=pltpu.CompilerParams(
            collective_id=0, has_side_effects=True, vmem_limit_bytes=56 * 1024 * 1024
        ),
        cost_estimate=pl.CostEstimate(
            flops=flops, bytes_accessed=8 * tokens * width, transcendentals=heads * tokens * BLOCK
        ),
        name="chained_attention",
    )(q, k, v, pace.reshape(1, heads), surplus.T, gain.reshape(1, width))


def solution(mesh):
    in_specs = (P("seq", "tp"), P("seq", "tp"), P("seq", "tp"), P("tp"), P("seq", "tp"), P("tp"))
    out_specs = (P("seq", "tp"), P("tp", "seq"))
    return jax.shard_map(
        functools.partial(on_device, mesh.shape["seq"], mesh.shape["tp"]),
        mesh=mesh, in_specs=in_specs, out_specs=out_specs, check_vma=False,
    )
```

profile of v0, /device:TPU:25, one launch (start us, length us, event | category | flops | bytes accessed | tf_op | source)
XLA Modules:
  0.0 42.7 jit_solution(3985339392760279734)
XLA Ops:
  0.6 38.2 %chained_attention.1 = (bf16[512,2048]{1,0:T(8,128)(2,1)}, f32[16,2048]{1,0:T(8,128)}) custom-call(bf16[512,2048]{1,0:T(8,128)(2,1)} %q_hbm.1, bf16[512,2048]{1,0:T(8,128)(2,1)} %k_hbm.1, bf16[512,2048]{1,0:T(8,128)(2,1)} %v_hbm.1, f32[1,16]{1,0:T(1,128)} %bitcast.5, f32[16,512]{1,0:T(8,128)} %bitcast.3, f32[1,2048]{1,0:T(1,128)} %bitcast.4), custom_call_target="tpu_custom_call" | custom-call | flops 2147483648 | bytes 8388608 | tf_op jit(solution)/shard_map/chained_attention/pallas_call | solution.py:408
  38.8 0.0 copy-start
  38.8 3.2 %copy.10 = bf16[512,2048]{1,0:T(8,128)(2,1)} copy(bf16[512,2048]{1,0:T(8,128)(2,1)} %get-tuple-element.4) | data formatting | bytes 4194304
  42.0 0.0 copy-done
  42.0 0.7 %copy.11 = f32[16,2048]{1,0:T(8,128)} copy(f32[16,2048]{1,0:T(8,128)S(1)} %copy-done) | data formatting | bytes 262144
Async XLA Ops:
  38.8 3.2 %copy-start = (f32[16,2048]{1,0:T(8,128)S(1)}, f32[16,2048]{1,0:T(8,128)}, u32[]{:S(2)}) copy-start(f32[16,2048]{1,0:T(8,128)} %get-tuple-element.5) | copy-start | bytes 393220
where the time goes:
time: 42.9 us; the launch traced here: 42.7 us
  Pallas kernels  38.2 us (89%)
  local copies, waits for them, and re-layouts  3.85 us (9%)
  between operations  0.65 us (2%)
    pallas_call x1, Pallas kernels, on_device(): pl.pallas_call(functools.partial(kernel, n, peers, heads, group), out_sha...  38.2 us
    unnamed x4, local copies, waits for them, and re-layouts  3.85 us

commit v1 on v0

--- a/solution.py
+++ b/solution.py
@@ -26,11 +26,11 @@
 
 def kernel(
     n, peers, heads, group,
-    q_hbm, k_hbm, v_hbm, pace_ref, surplus_ref, gain_ref,
-    out_hbm, final_ref,
-    qs, ks, vs, outs, acc, crow, erow, krow, dblock, first, local, theirs, prior, before, after, give,
+    q_hbm, k_hbm, v_hbm, pace_ref, surplus_ref,
+    acc, scale_ref, final_ref,
+    qs, ks, vs, crow, erow, krow, dblock, first, local, theirs, prior, before, after, give,
     dec, dec_theirs, fsend, frecv, squares,
-    load_sem, store_sem, dec_sem, l_send, l_recv, p_send, p_recv, x_send, x_recv,
+    load_sem, dec_sem, l_send, l_recv, p_send, p_recv, x_send, x_recv,
     f_send, f_recv, s_send, s_recv,
 ):
     tokens = q_hbm.shape[0]
@@ -85,9 +85,6 @@
             source.at[:, lanes(i)], target.at[i], load_sem.at[which, i]
         )
 
-    def store(i):
-        return pltpu.make_async_copy(outs.at[i], out_hbm.at[:, lanes(i)], store_sem.at[i])
-
     def span(i):
         return pl.ds(i * group, group)
 
@@ -135,8 +132,6 @@
     for i in range(chunks):
         load(0, i).start()
         load(1, i).start()
-    for i in range(chunks):
-        load(2, i).start()
 
     square = (heads, heads)
     diagonal = lax.broadcasted_iota(jnp.int32, square, 0) == lax.broadcasted_iota(
@@ -178,30 +173,35 @@
     pl.semaphore_wait(barrier, n + peers - 2)
     send_dec().start()
 
-    def make_local(i, carry):
-        load(0, i).wait()
-        load(1, i).wait()
-        for e in range(group):
-            h = i * group + e
+    def make_local(pair, carry):
+        for e in range(2):
+            h = pair * 2 + e
+            load(0, h).wait()
+            load(1, h).wait()
+            load(2, h).start()
+        for e in range(2):
+            h = pair * 2 + e
             row = krow[pl.ds(h, 1), :]
             state = None
             for b in range(blocks):
                 at = slice(b * BLOCK, (b + 1) * BLOCK)
-                kt = ks[i, at, e * HEAD_DIM : (e + 1) * HEAD_DIM].astype(F32).T
-                pair = jnp.dot(
-                    split(kt * row[:, at], 0), vs[i, at, e * HEAD_DIM : (e + 1) * HEAD_DIM],
-                    preferred_element_type=F32,
+                kt = ks[h, at, :].astype(F32).T
+                both = jnp.dot(
+                    split(kt * row[:, at], 0), vs[h, at, :], preferred_element_type=F32
                 )
-                fresh = pair[:HEAD_DIM] + pair[HEAD_DIM:]
+                fresh = both[:HEAD_DIM] + both[HEAD_DIM:]
                 state = fresh if b == 0 else dblock[b, pl.ds(h, 1), :] * state + fresh
                 if b < blocks - 1:
                     first[b, h] = state
             local[0, h], local[1, h] = halves(state)
-        send_local(i).start()
+        for e in range(2):
+            send_local(pair * 2 + e).start()
         return carry
 
-    lax.fori_loop(0, chunks, make_local, 0)
+    lax.fori_loop(0, heads // 2, make_local, 0)
     send_dec().wait_recv()
+
+    hold = jnp.maximum(chunks // 2 - 2 * g, 0)
 
     def chain(i):
         send_local(i).wait_recv()
@@ -230,7 +230,20 @@
 
         @pl.when(jnp.logical_not(is_first & (r == 1)))
         def _():
-            send_prior(i).start()
+            @pl.when(i >= hold)
+            def _():
+                send_prior(i - hold).start()
+
+            @pl.when(i == chunks - 1)
+            def _():
+                def rest(t, carry):
+                    @pl.when(t >= chunks - hold)
+                    def _():
+                        send_prior(t).start()
+
+                    return carry
+
+                lax.fori_loop(0, chunks, rest, 0)
 
         @pl.when(is_last)
         def _():
@@ -287,7 +300,7 @@
                     vs[i, at, cut], preferred_element_type=F32,
                 )
 
-    lag = jnp.minimum(g, chunks)
+    lag = jnp.minimum(3 * g, chunks)
 
     def middle(j, carry):
         @pl.when((j >= lag) & (j - lag < chunks))
@@ -300,7 +313,7 @@
 
         return carry
 
-    lax.fori_loop(0, chunks + min(groups - 1, chunks), middle, 0)
+    lax.fori_loop(0, chunks + min(3 * (groups - 1), chunks), middle, 0)
 
     def carried(i, sums):
         @pl.when(jnp.logical_not(is_first & (r == 0)))
@@ -344,7 +357,54 @@
     for step in range(1, peers):
         whole = whole + squares[step]
     scale = lax.rsqrt(whole / D + EPS)
-    scale = jnp.broadcast_to(scale, (HEAD_DIM, tokens)).T
+    scale_ref[...] = scale
+
+    def drain(i, carry):
+        send_local(i).wait_send()
+
+        @pl.when(jnp.logical_not(is_last))
+        def _():
+            send_after(i).wait_send()
+
+        @pl.when(jnp.logical_not(is_first & (r == 1)))
+        def _():
+            send_prior(i).wait_send()
+
+        @pl.when(is_last)
+        def _():
+            def sent(s, carry):
+                @pl.when(owner(s) != me)
+                def _():
+                    send_final(i, s).wait_send()
+
+                return carry
+
+            lax.fori_loop(0, groups, sent, 0)
+
+        @pl.when(jnp.logical_not(is_last & ((me * rows // piece) % 2 == r)))
+        def _():
+            send_final(i, 0).wait_recv()
+
+        return carry
+
+    lax.fori_loop(0, chunks, drain, 0)
+    send_dec().wait_send()
+    for step in range(1, peers):
+        send_squares(step).wait_send()
+    final_ref[...] = frecv[...]
+
+
+def norm_kernel(acc, scale_ref, gain_ref, final_in, out_hbm, final_ref, outs, store_sem):
+    heads, tokens = acc.shape[:2]
+    rows = final_in.shape[1]
+    wide = outs.shape[2]
+    group = wide // HEAD_DIM
+    scale = jnp.broadcast_to(scale_ref[...], (HEAD_DIM, tokens)).T
+
+    def store(i):
+        return pltpu.make_async_copy(
+            outs.at[i], out_hbm.at[:, pl.ds(pl.multiple_of(i * wide, wide), wide)], store_sem.at[i]
+        )
 
     def finish(i, carry):
         for e in range(group):
@@ -354,49 +414,21 @@
         store(i).start()
         return carry
 
-    lax.fori_loop(0, chunks, finish, 0)
+    lax.fori_loop(0, heads // group, finish, 0)
+    for at in range(rows):
+        final_ref[:, at * HEAD_DIM : (at + 1) * HEAD_DIM] = final_in[:, at, :]
 
     def drain(i, carry):
-        send_local(i).wait_send()
-
-        @pl.when(jnp.logical_not(is_last))
-        def _():
-            send_after(i).wait_send()
-
-        @pl.when(jnp.logical_not(is_first & (r == 1)))
-        def _():
-            send_prior(i).wait_send()
-
-        @pl.when(is_last)
-        def _():
-            def sent(s, carry):
-                @pl.when(owner(s) != me)
-                def _():
-                    send_final(i, s).wait_send()
-
-                return carry
-
-            lax.fori_loop(0, groups, sent, 0)
-
-        @pl.when(jnp.logical_not(is_last & ((me * rows // piece) % 2 == r)))
-        def _():
-            send_final(i, 0).wait_recv()
-
         store(i).wait()
         return carry
 
-    lax.fori_loop(0, chunks, drain, 0)
-    send_dec().wait_send()
-    for step in range(1, peers):
-        send_squares(step).wait_send()
-    for at in range(rows):
-        final_ref[:, at * HEAD_DIM : (at + 1) * HEAD_DIM] = frecv[:, at, :]
+    lax.fori_loop(0, heads // group, drain, 0)
 
 
 def on_device(n, peers, q, k, v, pace, surplus, gain):
     tokens, width = q.shape
     heads = pace.shape[0]
-    group = 2
+    group = 1
     chunks = heads // group
     blocks = tokens // BLOCK
     groups = n // 2
@@ -405,24 +437,20 @@
     dma = pltpu.SemaphoreType.DMA
     half = (heads, HALF, HEAD_DIM)
     flops = 2 * heads * tokens * HEAD_DIM * (2 * BLOCK + 4 * HEAD_DIM)
-    return pl.pallas_call(
+    acc, scale, final = pl.pallas_call(
         functools.partial(kernel, n, peers, heads, group),
         out_shape=(
-            jax.ShapeDtypeStruct((tokens, width), BF16),
-            jax.ShapeDtypeStruct((heads, rows * HEAD_DIM), F32),
+            vmem((heads, tokens, HEAD_DIM), F32),
+            vmem((1, tokens), F32),
+            vmem((heads, rows, HEAD_DIM), F32),
         ),
         in_specs=[pl.BlockSpec(memory_space=pl.ANY)] * 3
-        + [pl.BlockSpec(memory_space=pltpu.VMEM)] * 3,
-        out_specs=(
-            pl.BlockSpec(memory_space=pl.ANY),
-            pl.BlockSpec(memory_space=pltpu.VMEM),
-        ),
+        + [pl.BlockSpec(memory_space=pltpu.VMEM)] * 2,
+        out_specs=[pl.BlockSpec(memory_space=pltpu.VMEM)] * 3,
         scratch_shapes=[
             vmem((chunks, tokens, group * HEAD_DIM), BF16),
             vmem((chunks, tokens, group * HEAD_DIM), BF16),
             vmem((chunks, tokens, group * HEAD_DIM), BF16),
-            vmem((chunks, tokens, group * HEAD_DIM), BF16),
-            vmem((heads, tokens, HEAD_DIM), F32),
             vmem((heads, tokens), F32),
             vmem((heads, tokens), F32),
             vmem((heads, tokens), F32),
@@ -440,7 +468,6 @@
             vmem((heads, rows, HEAD_DIM), F32),
             vmem((peers, 1, tokens), F32),
             dma((3, chunks)),
-            dma((chunks,)),
             dma((2,)),
             dma((chunks,)),
             dma((chunks,)),
@@ -454,13 +481,31 @@
             dma((peers,)),
         ],
         compiler_params=pltpu.CompilerParams(
-            collective_id=0, has_side_effects=True, vmem_limit_bytes=56 * 1024 * 1024
+            collective_id=0, has_side_effects=True, vmem_limit_bytes=58 * 1024 * 1024
         ),
         cost_estimate=pl.CostEstimate(
             flops=flops, bytes_accessed=8 * tokens * width, transcendentals=heads * tokens * BLOCK
         ),
         name="chained_attention",
-    )(q, k, v, pace.reshape(1, heads), surplus.T, gain.reshape(1, width))
+    )(q, k, v, pace.reshape(1, heads), surplus.T)
+    return pl.pallas_call(
+        norm_kernel,
+        out_shape=(
+            jax.ShapeDtypeStruct((tokens, width), BF16),
+            jax.ShapeDtypeStruct((heads, rows * HEAD_DIM), F32),
+        ),
+        in_specs=[pl.BlockSpec(memory_space=pltpu.VMEM)] * 4,
+        out_specs=(
+            pl.BlockSpec(memory_space=pl.ANY),
+            pl.BlockSpec(memory_space=pltpu.VMEM),
+        ),
+        scratch_shapes=[vmem((heads // 2, tokens, 2 * HEAD_DIM), BF16), dma((heads // 2,))],
+        compiler_params=pltpu.CompilerParams(vmem_limit_bytes=16 * 1024 * 1024),
+        cost_estimate=pl.CostEstimate(
+            flops=3 * tokens * width, bytes_accessed=6 * tokens * width, transcendentals=0
+        ),
+        name="norm",
+    )(acc, scale, gain.reshape(1, width), final)
 
 
 def solution(mesh):

time: 42.9 us -> 40.6 us (0.946)
  local copies, waits for them, and re-layouts: 3.85 us -> 0.01 us
  Pallas kernels: 38.2 us -> 39.8 us
    unnamed x4 -> x2, local copies, waits for them, and re-layouts: 3.85 us -> 0.01 us
    pallas_call x0 -> x1, Pallas kernels: none -> 2.22 us  [on_device(): pl.pallas_call(norm_kernel, out_shape=(jax.ShapeDtypeStruct((tokens, widt...]
    pallas_call x1, Pallas kernels: 38.2 us -> 37.6 us  [on_device(): pl.pallas_call(functools.partial(kernel, n, peers, heads, group), out_sha...]
where the time goes in v1:
time: 40.6 us; the launch traced here: 40.5 us
  Pallas kernels  39.8 us (98%)
  between operations  0.66 us (2%)
    pallas_call x1, Pallas kernels, on_device(): pl.pallas_call(functools.partial(kernel, n, peers, heads, group), out_sha...  37.6 us
    pallas_call x1, Pallas kernels, on_device(): pl.pallas_call(norm_kernel, out_shape=(jax.ShapeDtypeStruct((tokens, widt...  2.22 us

profile of v1, /device:TPU:25, one launch (start us, length us, event | category | flops | bytes accessed | tf_op | source)
XLA Modules:
  0.0 40.5 jit_solution(2044122489678977921)
XLA Ops:
  0.6 0.0 copy-start
  0.6 37.6 %chained_attention.1 = (f32[16,512,128]{2,1,0:T(8,128)S(1)}, f32[1,512]{1,0:T(1,128)S(1)}, f32[16,16,128]{2,1,0:T(8,128)S(1)}) custom-call(bf16[512,2048]{1,0:T(8,128)(2,1)} %q_hbm.1, bf16[512,2048]{1,0:T(8,128)(2,1)} %k_hbm.1, bf16[512,2048]{1,0:T(8,128)(2,1)} %v_hbm.1, f32[1,16]{1,0:T(1,128)} %bitcast.5, f32[16,512]{1,0:T(8,128)} %bitcast.4), custom_call_target="tpu_custom_call" | custom-call | flops 2147483648 | bytes 8388608 | tf_op jit(solution)/shard_map/chained_attention/pallas_call | solution.py:440
  38.2 0.0 copy-done
  38.2 2.2 %norm.1 = (bf16[512,2048]{1,0:T(8,128)(2,1)}, f32[16,2048]{1,0:T(8,128)}) custom-call(f32[16,512,128]{2,1,0:T(8,128)S(1)} %get-tuple-element.5.acc, f32[1,512]{1,0:T(1,128)S(1)} %get-tuple-element.6.scale_ref, f32[1,2048]{1,0:T(1,128)S(1)} %bitcast.3, f32[16,16,128]{2,1,0:T(8,128)S(1)} %get-tuple-element.7.final_in), custom_call_target="tpu_custom_call" | custom-call | flops 3145728 | bytes 6291456 | tf_op jit(solution)/shard_map/norm/pallas_call | solution.py:491
Async XLA Ops:
  0.6 37.6 %copy-start = (f32[2048]{0:T(1024)S(1)}, f32[2048]{0:T(1024)}, u32[]{:S(2)}) copy-start(f32[2048]{0:T(1024)} %param.11) | copy-start | bytes 24580
